TPU v7x, 32 devices: a whole 2x2x4 slice. The times are simulated.
32 devices in a mesh: dp: 8 (over y, x, core), pipe: 4 (over z).
Axes of the slice: x: 2, y: 2, z: 4, core: 2. Of those that a mesh axis runs over, the one named last changes fastest.
Arguments:
- latents_in: bfloat16 [3, 512, 3072], P(None, 'dp'), may hold values from -6 to 6
- context_cache: bfloat16 [2, 256, 3072], P(None, 'dp'), may hold values from -6 to 6
- w_qk: bfloat16 [4, 3072, 3072], P('pipe', 'dp'), may hold values from -2.75 to 2.75
- w_v: bfloat16 [4, 3072, 1536], P('pipe'), may hold values from -0.109375 to 0.109375
- w_out: bfloat16 [4, 3072, 1536], P('pipe'), may hold values from -0.15625 to 0.15625
- tile_mask: int32 [3, 8, 2], P(None, 'dp'), may hold values from 0 to 1, as said below
- out_cotangent: bfloat16 [4, 3, 512, 3072], P('pipe', None, 'dp'), may hold values from -6 to 6
Outputs:
- grad_out_proj: float32 [4, 3072, 1536], P('pipe', 'dp')
Inputs may be any that keep to these rules, and one draw needn't show every extreme that they name: `tile_mask`: for the r-th tile of a block, key tile r + 1 is always allowed and key tiles above r + 1 never; key tile 0 is the 32 context rows.
All inputs are finite; a program needn't handle non-finite values.
Results may differ from a plain program's by a relative error of at most 0.018.
Values may be sent and summed in bfloat16 or wider, within the bound.
A program may use at most 128 MiB of HBM per device.

v0:
```python
import jax
import jax.numpy as jnp
import numpy as np
from jax import lax
from jax.sharding import PartitionSpec as P

HEADS = 12
HDIM = 128
TILE = 64
MB = 3
LAG = 2


def passed_along(block, axis, distance):
    devices = range(lax.axis_size(axis))
    route = [((i - distance) % len(devices), i) for i in devices]
    return lax.ppermute(block, axis, route)


def allowed_keys(tile_block, ctx_rows):
    columns = jnp.concatenate(
        [
            jnp.repeat(tile_block[:, :1], ctx_rows, axis=1),
            jnp.repeat(tile_block[:, 1:], TILE, axis=1),
        ],
        axis=1,
    )
    return jnp.repeat(columns, TILE, axis=0) == 1


def attend(hidden, context, tile_block, weights_q, weights_k, weights_v, weights_out):
    ctx_rows = context.shape[0]
    tok_rows = hidden.shape[0]
    heads_width = weights_v.shape[1]
    joined = jnp.concatenate([context, hidden], axis=0).astype(jnp.float32)
    normed = (joined * lax.rsqrt(jnp.mean(joined * joined, axis=-1, keepdims=True) + 1e-06)).astype(
        jnp.bfloat16
    )
    queries = jnp.dot(normed[ctx_rows:], weights_q, preferred_element_type=jnp.float32).astype(
        jnp.bfloat16
    )
    key_rows = jnp.dot(normed, weights_k, preferred_element_type=jnp.float32).astype(jnp.bfloat16)
    value_rows = jnp.dot(normed, weights_v, preferred_element_type=jnp.float32).astype(jnp.bfloat16)
    query_heads = queries.reshape(tok_rows, HEADS, HDIM)
    key_heads = key_rows.reshape(ctx_rows + tok_rows, HEADS, HDIM)
    value_heads = value_rows.reshape(ctx_rows + tok_rows, HEADS, HDIM)
    scores = jnp.einsum(
        "qhd,khd->hqk", query_heads, key_heads, preferred_element_type=jnp.float32
    ) * HDIM ** (-0.5)
    allowed = allowed_keys(tile_block, ctx_rows)
    scores = jnp.where(allowed[None], scores, -1e30)
    largest = jnp.max(scores, axis=-1, keepdims=True)
    exponent = jnp.exp(scores - largest)
    attention = (exponent / jnp.sum(exponent, axis=-1, keepdims=True)).astype(jnp.bfloat16)
    mixed_heads = jnp.einsum(
        "hqk,khd->qhd", attention, value_heads, preferred_element_type=jnp.float32
    )
    mixed_heads = mixed_heads.astype(jnp.bfloat16).reshape(tok_rows, heads_width)
    update = lax.dot_general(
        mixed_heads, weights_out, (((1,), (1,)), ((), ())), preferred_element_type=jnp.float32
    )
    result = (hidden.astype(jnp.float32) + update).astype(jnp.bfloat16)
    return (result, mixed_heads)


def local(latents_in, context_cache, w_qk, w_v, w_out, tile_mask, out_cotangent):
    segments = lax.axis_size("pipe")
    segment_index = lax.axis_index("pipe")
    tok_rows = latents_in.shape[1]
    model_width = latents_in.shape[2]
    ctx_rows = context_cache.shape[1]
    heads_width = w_v.shape[2]
    weights_q, weights_k = (
        lax.all_gather(w_qk[0][:, :heads_width], "dp", axis=0, tiled=True),
        lax.all_gather(w_qk[0][:, heads_width:], "dp", axis=0, tiled=True),
    )
    weights_v = w_v[0]
    weights_out = w_out[0]
    cotangent_local = out_cotangent[0]
    starts = [microbatch // LAG * segments + microbatch % LAG for microbatch in range(MB)]
    moments = starts[-1] + segments
    plan_table = np.full((moments, segments), -1, np.int32)
    for microbatch in range(MB):
        for section in range(segments):
            plan_table[starts[microbatch] + section, section] = microbatch
    roster = jnp.asarray(plan_table)
    records = jnp.zeros((MB, tok_rows, heads_width), jnp.bfloat16)
    incoming = jnp.zeros((tok_rows, model_width), jnp.bfloat16)
    incoming_ctx = jnp.zeros((ctx_rows, model_width), jnp.bfloat16)
    leading = segment_index == 0

    def advance(operands):
        hidden, context, chosen, kept = operands
        result, mixed_heads = attend(
            hidden, context, tile_mask[chosen], weights_q, weights_k, weights_v, weights_out
        )
        return (result, lax.dynamic_update_slice_in_dim(kept, mixed_heads[None], chosen, 0))

    def standby(operands):
        return (operands[0], operands[3])

    for moment in range(moments):
        current = roster[moment, segment_index]
        chosen = jnp.maximum(current, 0)
        hidden = jnp.where(leading, latents_in[chosen], incoming)
        first_context = jnp.where(
            chosen < LAG,
            context_cache[jnp.minimum(chosen, LAG - 1)],
            incoming[tok_rows - ctx_rows :],
        )
        context = jnp.where(leading, first_context, incoming_ctx)
        result, records = lax.cond(
            current >= 0, advance, standby, (hidden, context, chosen, records)
        )
        if moment + 1 < moments:
            incoming, incoming_ctx = passed_along((result, context), "pipe", 1)
    cotangent_rows = cotangent_local.reshape(MB * tok_rows, model_width)
    mixed_rows = records.reshape(MB * tok_rows, heads_width)
    gradient = lax.psum_scatter(
        lax.dot_general(
            cotangent_rows, mixed_rows, (((0,), (0,)), ((), ())), preferred_element_type=jnp.float32
        ).astype(jnp.bfloat16),
        "dp",
        scatter_dimension=0,
        tiled=True,
    ).astype(jnp.float32)
    return gradient[None]


def solution(mesh):
    in_specs = (
        P(None, "dp", None),
        P(None, "dp", None),
        P("pipe", "dp", None),
        P("pipe", None, None),
        P("pipe", None, None),
        P(None, "dp", None),
        P("pipe", None, "dp", None),
    )
    out_specs = P("pipe", "dp", None)
    return jax.shard_map(local, mesh=mesh, in_specs=in_specs, out_specs=out_specs, check_vma=False)
```

profile of v0, /device:TPU:25, one launch (start us, length us, event | category | flops | bytes accessed | tf_op | source)
XLA Modules:
  0.0 551.6 jit_solution(14622836060370693701)
XLA Ops:
  6.5 3.3 fusion.191
  12.7 57.5 %all-gather.3.cloned.1.call-done = bf16[3072,1536]{1,0:T(8,128)(2,1)} async-done(((bf16[384,1536]{1,0:T(8,128)(2,1)}), bf16[3072,1536]{1,0:T(8,128)(2,1)}) %all-gather.3.cloned.1.call-update) | async-done | bytes 9437200 | tf_op jit(solution)/shard_map/all_gather | solution.py:74
  70.3 60.7 %all-gather.5.cloned.1.call-done = bf16[3072,1536]{1,0:T(8,128)(2,1)} async-done(((bf16[384,1536]{1,0:T(8,128)(2,1)}), bf16[3072,1536]{1,0:T(8,128)(2,1)}) %all-gather.5.cloned.1.call-update) | async-done | bytes 9437200 | tf_op jit(solution)/shard_map/all_gather | solution.py:75
  131.9 27.8 %collective-permute-start = (bf16[64,3072]{1,0:T(8,128)(2,1)S(1)}, bf16[64,3072]{1,0:T(8,128)(2,1)}, u32[]{:S(2)}, u32[]{:S(2)}) collective-permute-start(bf16[64,3072]{1,0:T(8,128)(2,1)S(1)} %get-tuple-element.407), channel_id=1, source_target_pairs={{3,0},{0,1},{1,2},{2,3},{7,4},{4,5},{5,6},{6,7},{11,8},{8,9},{9,10... | collective-permute-start | bytes 1179656 | tf_op jit(solution)/shard_map/ppermute | solution.py:17
  161.1 6.8 %collective-permute-done = bf16[64,3072]{1,0:T(8,128)(2,1)} collective-permute-done((bf16[64,3072]{1,0:T(8,128)(2,1)S(1)}, bf16[64,3072]{1,0:T(8,128)(2,1)}, u32[]{:S(2)}, u32[]{:S(2)}) %collective-permute-start) | collective-permute-done | bytes 393248 | tf_op jit(solution)/shard_map/ppermute | solution.py:17
  167.9 1.0 bitcast_select_fusion.2
  169.0 3.2 collective-permute-done.1
  173.4 31.6 %collective-permute-start.2 = (bf16[64,3072]{1,0:T(8,128)(2,1)S(1)}, bf16[64,3072]{1,0:T(8,128)(2,1)}, u32[]{:S(2)}, u32[]{:S(2)}) collective-permute-start(bf16[64,3072]{1,0:T(8,128)(2,1)S(1)} %get-tuple-element.409), channel_id=1, source_target_pairs={{3,0},{0,1},{1,2},{2,3},{7,4},{4,5},{5,6},{6,7},{11,8},{8,9},{9,10... | collective-permute-start | bytes 1179656 | tf_op jit(solution)/shard_map/ppermute | solution.py:17
  206.4 5.9 %collective-permute-done.2 = bf16[64,3072]{1,0:T(8,128)(2,1)} collective-permute-done((bf16[64,3072]{1,0:T(8,128)(2,1)S(1)}, bf16[64,3072]{1,0:T(8,128)(2,1)}, u32[]{:S(2)}, u32[]{:S(2)}) %collective-permute-start.2) | collective-permute-done | bytes 393248 | tf_op jit(solution)/shard_map/ppermute | solution.py:17
  212.3 1.0 bitcast_select_fusion.3
  213.4 3.2 collective-permute-done.3
  216.6 1.0 fusion.173
  217.9 4.1 collective-permute-start.4
  223.0 26.1 %collective-permute-start.5 = (bf16[32,3072]{1,0:T(8,128)(2,1)S(1)}, bf16[32,3072]{1,0:T(8,128)(2,1)S(1)}, u32[]{:S(2)}, u32[]{:S(2)}) collective-permute-start(bf16[32,3072]{1,0:T(8,128)(2,1)S(1)} %fusion.173), channel_id=1, source_target_pairs={{3,0},{0,1},{1,2},{2,3},{7,4},{4,5},{5,6},{6,7},{11,8},{8,9},{9,10... | collective-permute-start | bytes 589832 | tf_op jit(solution)/shard_map/ppermute | solution.py:17
  249.1 3.6 collective-permute-done.4
  252.7 1.0 bitcast_select_fusion.4
  253.7 3.1 collective-permute-done.5
  256.8 1.0 fusion.172
  257.8 28.2 %conditional.11 = ((bf16[64,3072]{1,0:T(8,128)(2,1)S(1)}, bf16[3,64,1536]{2,1,0:T(8,128)(2,1)})) conditional(s32[]{:T(128)} %bitcast.42, (bf16[64,3072]{1,0:T(8,128)(2,1)S(1)}, bf16[3,64,1536]{2,1,0:T(8,128)(2,1)}) %tuple.88, (bf16[64,3072]{1,0:T(8,128)(2,1)S(1)}, bf16[32,3072]{1,0:T(8,128)(2,1)S(1)}, bf16[3072,1536]{1,0:T(8,128)(2,1)}, ...), branch_computations={%region_15.16_spmd, %region_16.20_spmd} | conditional | flops 3062784768 | bytes 103719160 | solution.py:112
  258.8 6.2 %fusion.70 = bf16[12,12,8,128]{3,2,1,0:T(8,128)(2,1)} fusion(bf16[96,3072]{1,0:T(8,128)(2,1)S(1)} %fusion.69, bf16[3072,1536]{1,0:T(8,128)(2,1)} %get-tuple-element.344), kind=kOutput, calls=%fused_computation.120 | convolution fusion | flops 906117120 | bytes 10321920 | tf_op jit(solution)/shard_map/cond/branch_1_fun/dot_general | solution.py:43
  265.0 2.3 fusion.71
  268.1 1.7 fusion.72
  271.8 1.3 fusion.67
  274.1 2.6 convolution_convert_fusion.15
  276.7 6.6 %fusion.64 = bf16[64,3072]{1,0:T(8,128)(2,1)S(1)} fusion(bf16[3072,1536]{1,0:T(8,128)(2,1)} %get-tuple-element.349, bf16[64,3072]{1,0:T(8,128)(2,1)S(1)} %get-tuple-element.342, bf16[12,128,64]{1,2,0:T(8,128)(2,1)S(1)} %convolution_convert_fusion.15), kind=kOutput, calls=%fused_computation.107 | convolution fusion | flops 604569600 | bytes 10420224 | tf_op jit(solution)/shard_map/cond/branch_1_fun/dot_general | solution.py:59
  284.2 1.1 reshape.350
  287.4 8.0 %collective-permute-done.6 = bf16[64,3072]{1,0:T(8,128)(2,1)} collective-permute-done((bf16[64,3072]{1,0:T(8,128)(2,1)S(1)}, bf16[64,3072]{1,0:T(8,128)(2,1)}, u32[]{:S(2)}, u32[]{:S(2)}) %collective-permute-start.6) | collective-permute-done | bytes 393248 | tf_op jit(solution)/shard_map/ppermute | solution.py:17
  295.4 1.0 bitcast_select_fusion.5
  296.5 3.2 collective-permute-done.7
  299.6 1.0 fusion.171
  300.6 27.8 %conditional.12 = ((bf16[64,3072]{1,0:T(8,128)(2,1)S(1)}, bf16[3,64,1536]{2,1,0:T(8,128)(2,1)})) conditional(s32[]{:T(128)} %bitcast.39, (bf16[64,3072]{1,0:T(8,128)(2,1)S(1)}, bf16[3,64,1536]{2,1,0:T(8,128)(2,1)}) %tuple.90, (bf16[64,3072]{1,0:T(8,128)(2,1)S(1)}, bf16[32,3072]{1,0:T(8,128)(2,1)S(1)}, bf16[3072,1536]{1,0:T(8,128)(2,1)}, ...), branch_computations={%region_20.21_spmd, %region_21.25_spmd} | conditional | flops 3062784768 | bytes 103719160 | solution.py:112
  301.2 6.2 %fusion.91 = bf16[12,12,8,128]{3,2,1,0:T(8,128)(2,1)} fusion(bf16[96,3072]{1,0:T(8,128)(2,1)S(1)} %fusion.90, bf16[3072,1536]{1,0:T(8,128)(2,1)} %get-tuple-element.353), kind=kOutput, calls=%fused_computation.155 | convolution fusion | flops 906117120 | bytes 10321920 | tf_op jit(solution)/shard_map/cond/branch_1_fun/dot_general | solution.py:43
  307.4 2.3 fusion.92
  310.5 1.7 fusion.93
  314.2 1.3 fusion.88
  316.5 2.6 convolution_convert_fusion.19
  319.1 6.6 %fusion.85 = bf16[64,3072]{1,0:T(8,128)(2,1)S(1)} fusion(bf16[3072,1536]{1,0:T(8,128)(2,1)} %get-tuple-element.358, bf16[64,3072]{1,0:T(8,128)(2,1)S(1)} %get-tuple-element.351, bf16[12,128,64]{1,2,0:T(8,128)(2,1)S(1)} %convolution_convert_fusion.19), kind=kOutput, calls=%fused_computation.142 | convolution fusion | flops 604569600 | bytes 10420224 | tf_op jit(solution)/shard_map/cond/branch_1_fun/dot_general | solution.py:59
  326.6 1.1 reshape.356
  328.4 1.4 collective-permute-start.8
  331.2 5.0 collective-permute-done.8
  336.2 1.0 bitcast_select_fusion.6
  337.3 3.2 collective-permute-done.9
  340.4 1.0 fusion.170
  341.6 3.6 collective-permute-start.10
  346.4 26.1 %collective-permute-start.11 = (bf16[32,3072]{1,0:T(8,128)(2,1)S(1)}, bf16[32,3072]{1,0:T(8,128)(2,1)S(1)}, u32[]{:S(2)}, u32[]{:S(2)}) collective-permute-start(bf16[32,3072]{1,0:T(8,128)(2,1)S(1)} %fusion.170), channel_id=1, source_target_pairs={{3,0},{0,1},{1,2},{2,3},{7,4},{4,5},{5,6},{6,7},{11,8},{8,9},{9,10... | collective-permute-start | bytes 589832 | tf_op jit(solution)/shard_map/ppermute | solution.py:17
  372.4 1.0 bitcast_select_fusion.7
  373.5 1.6 collective-permute-done.11
  375.0 1.0 fusion.169
  376.3 5.8 %collective-permute-start.12 = (bf16[64,3072]{1,0:T(8,128)(2,1)S(1)}, bf16[64,3072]{1,0:T(8,128)(2,1)}, u32[]{:S(2)}, u32[]{:S(2)}) collective-permute-start(bf16[64,3072]{1,0:T(8,128)(2,1)S(1)} %get-tuple-element.420), channel_id=1, source_target_pairs={{3,0},{0,1},{1,2},{2,3},{7,4},{4,5},{5,6},{6,7},{11,8},{8,9},{9,10... | collective-permute-start | bytes 1179656 | tf_op jit(solution)/shard_map/ppermute | solution.py:17
  382.1 2.3 collective-permute-start.13
  385.1 34.9 %collective-permute-done.13 = bf16[32,3072]{1,0:T(8,128)(2,1)S(1)} collective-permute-done((bf16[32,3072]{1,0:T(8,128)(2,1)S(1)}, bf16[32,3072]{1,0:T(8,128)(2,1)S(1)}, u32[]{:S(2)}, u32[]{:S(2)}) %collective-permute-start.13) | collective-permute-done | bytes 196640 | tf_op jit(solution)/shard_map/ppermute | solution.py:17
  420.8 19.3 %conditional.15 = (bf16[192,1536]{1,0:T(8,128)(2,1)}) conditional(s32[]{:T(128)} %convert_element_type.307, bf16[3,64,1536]{2,1,0:T(8,128)(2,1)} %get-tuple-element.419, (s32[]{:T(128)}, bf16[2,32,3072]{2,1,0:T(8,128)(2,1)S(1)}, bf16[64,3072]{1,0:T(8,128)(2,1)}, pred[32,3072]{1,0:T(8,128)(4,1)S(1)}, bf16[32,3072]{1,0:T(8,128)(2,1)}, ...), branch_computations={%region_35.36_spmd, %region_36.40_spmd} | conditional | flops 2458608384 | bytes 94380248 | solution.py:112
  421.8 1.1 bitcast_select_fusion
  422.8 1.1 fusion.143
  424.3 5.4 fusion.132
  430.5 1.6 fusion.133
  433.4 1.7 fusion.135
  437.7 1.4 fusion.134
  440.0 6.1 %fusion.168 = bf16[3072,1536]{0,1:T(8,128)(2,1)} fusion(bf16[192,1536]{1,0:T(8,128)(2,1)} %get-tuple-element.422, bf16[192,3072]{1,0:T(8,128)(2,1)S(1)} %bitcast.336), kind=kOutput, calls=%fused_computation.282 | convolution fusion | flops 1816657920 | bytes 11206656 | tf_op jit(solution)/shard_map/dot_general | solution.py:120
  446.2 12.6 %copy.138 = bf16[3072,1536]{1,0:T(8,128)(2,1)} copy(bf16[3072,1536]{0,1:T(8,128)(2,1)} %fusion.168) | data formatting | bytes 18874368
  458.8 80.2 %reduce-scatter.4.cloned.1.call-done = bf16[384,1536]{1,0:T(8,128)(2,1)} async-done(((bf16[3072,1536]{1,0:T(8,128)(2,1)}), bf16[384,1536]{1,0:T(8,128)(2,1)}) %reduce-scatter.4.cloned.1.call-update) | async-done | bytes 1179664
  539.1 2.4 copy.139
  541.4 1.4 bitcast_convert_fusion
  542.9 2.0 copy.137
  (118 shorter events, 23.6 us)
Async XLA Ops:
  6.5 433.5 %copy-start = (bf16[1,3,64,3072]{3,2,1,0:T(8,128)(2,1)S(1)}, bf16[1,3,64,3072]{3,2,1,0:T(8,128)(2,1)}, u32[]{:S(2)}) copy-start(bf16[1,3,64,3072]{3,2,1,0:T(8,128)(2,1)} %param.30) | copy-start | bytes 3538948
  6.5 63.7 %all-gather.3.cloned.1.call-start = ((), (), s32[]{:S(2)}) async-start(), calls=%async_computation.1 | async-start | bytes 10616832 | tf_op jit(solution)/shard_map/all_gather | solution.py:74
  9.8 0.8 copy-start.12
  9.8 2.8 copy-start.2
  9.8 2.8 copy-start.1
  9.9 121.1 %all-gather.5.cloned.1.call-start = ((), (), s32[]{:S(2)}) async-start(), calls=%async_computation.2 | async-start | bytes 10616832 | tf_op jit(solution)/shard_map/all_gather | solution.py:75
  9.9 121.1 %copy-start.11 = (s32[3,1,2]{0,2,1:T(2,128)S(1)}, s32[3,1,2]{0,2,1:T(2,128)}, u32[]{:S(2)}) copy-start(s32[3,1,2]{0,2,1:T(2,128)} %param.29) | copy-start | bytes 76
  10.6 528.4 %reduce-scatter.4.cloned.1.call-start = ((), (), s32[]{:S(2)}) async-start(), calls=%async_computation.3 | async-start | bytes 10616832
  131.9 36.1 %collective-permute-start = (bf16[64,3072]{1,0:T(8,128)(2,1)S(1)}, bf16[64,3072]{1,0:T(8,128)(2,1)}, u32[]{:S(2)}, u32[]{:S(2)}) collective-permute-start(bf16[64,3072]{1,0:T(8,128)(2,1)S(1)} %get-tuple-element.407), channel_id=1, source_target_pairs={{3,0},{0,1},{1,2},{2,3},{7,4},{4,5},{5,6},{6,7},{11,8},{8,9},{9,10... | collective-permute-start | bytes 1179656 | tf_op jit(solution)/shard_map/ppermute | solution.py:17
  159.7 12.5 %collective-permute-start.1 = (bf16[32,3072]{1,0:T(8,128)(2,1)S(1)}, bf16[32,3072]{1,0:T(8,128)(2,1)S(1)}, u32[]{:S(2)}, u32[]{:S(2)}) collective-permute-start(bf16[32,3072]{1,0:T(8,128)(2,1)S(1)} %select_bitcast_fusion.1), channel_id=1, source_target_pairs={{3,0},{0,1},{1,2},{2,3},{7,4},{4,5},{5,6},{6,7},{11,8},{8,9},{9,10... | collective-permute-start | bytes 589832 | tf_op jit(solution)/shard_map/ppermute | solution.py:17
  173.4 38.9 %collective-permute-start.2 = (bf16[64,3072]{1,0:T(8,128)(2,1)S(1)}, bf16[64,3072]{1,0:T(8,128)(2,1)}, u32[]{:S(2)}, u32[]{:S(2)}) collective-permute-start(bf16[64,3072]{1,0:T(8,128)(2,1)S(1)} %get-tuple-element.409), channel_id=1, source_target_pairs={{3,0},{0,1},{1,2},{2,3},{7,4},{4,5},{5,6},{6,7},{11,8},{8,9},{9,10... | collective-permute-start | bytes 1179656 | tf_op jit(solution)/shard_map/ppermute | solution.py:17
  206.4 10.2 %collective-permute-start.3 = (bf16[32,3072]{1,0:T(8,128)(2,1)S(1)}, bf16[32,3072]{1,0:T(8,128)(2,1)S(1)}, u32[]{:S(2)}, u32[]{:S(2)}) collective-permute-start(bf16[32,3072]{1,0:T(8,128)(2,1)S(1)} %fusion.174), channel_id=1, source_target_pairs={{3,0},{0,1},{1,2},{2,3},{7,4},{4,5},{5,6},{6,7},{11,8},{8,9},{9,10... | collective-permute-start | bytes 589832 | tf_op jit(solution)/shard_map/ppermute | solution.py:17
  217.9 34.8 %collective-permute-start.4 = (bf16[64,3072]{1,0:T(8,128)(2,1)S(1)}, bf16[64,3072]{1,0:T(8,128)(2,1)}, u32[]{:S(2)}, u32[]{:S(2)}) collective-permute-start(bf16[64,3072]{1,0:T(8,128)(2,1)S(1)} %get-tuple-element.411), channel_id=1, source_target_pairs={{3,0},{0,1},{1,2},{2,3},{7,4},{4,5},{5,6},{6,7},{11,8},{8,9},{9,10... | collective-permute-start | bytes 1179656 | tf_op jit(solution)/shard_map/ppermute | solution.py:17
  223.0 33.8 %collective-permute-start.5 = (bf16[32,3072]{1,0:T(8,128)(2,1)S(1)}, bf16[32,3072]{1,0:T(8,128)(2,1)S(1)}, u32[]{:S(2)}, u32[]{:S(2)}) collective-permute-start(bf16[32,3072]{1,0:T(8,128)(2,1)S(1)} %fusion.173), channel_id=1, source_target_pairs={{3,0},{0,1},{1,2},{2,3},{7,4},{4,5},{5,6},{6,7},{11,8},{8,9},{9,10... | collective-permute-start | bytes 589832 | tf_op jit(solution)/shard_map/ppermute | solution.py:17
  258.6 6.4 %slice-start.9 = ((s8[9437184]{0:T(1024)(128)(4,1)}), s8[4194304]{0:T(1024)(128)(4,1)S(1)}, s32[]{:S(2)}) async-start(s8[9437184]{0:T(1024)(128)(4,1)} %bitcast.351), calls=%async_computation.13 | async-start | bytes 8388608 | tf_op jit(solution)/shard_map/cond
  258.8 6.2 %slice-start.10 = ((s8[9437184]{0:T(1024)(128)(4,1)}), s8[4194304]{0:T(1024)(128)(4,1)S(1)}, s32[]{:S(2)}) async-start(s8[9437184]{0:T(1024)(128)(4,1)} %bitcast.351), calls=%async_computation.14 | async-start | bytes 8388608 | tf_op jit(solution)/shard_map/cond
  258.8 6.2 %slice-start.11 = ((s8[9437184]{0:T(1024)(128)(4,1)}), s8[1048576]{0:T(1024)(128)(4,1)S(1)}, s32[]{:S(2)}) async-start(s8[9437184]{0:T(1024)(128)(4,1)} %bitcast.351), calls=%async_computation.15 | async-start | bytes 2097152 | tf_op jit(solution)/shard_map/cond
  258.8 8.6 %slice-start.33 = ((s8[9437184]{0:T(1024)(128)(4,1)}), s8[4194304]{0:T(1024)(128)(4,1)S(1)}, s32[]{:S(2)}) async-start(s8[9437184]{0:T(1024)(128)(4,1)} %bitcast.367), calls=%async_computation.37 | async-start | bytes 8388608 | tf_op jit(solution)/shard_map/cond
  258.8 8.8 %slice-start.34 = ((s8[9437184]{0:T(1024)(128)(4,1)}), s8[4194304]{0:T(1024)(128)(4,1)S(1)}, s32[]{:S(2)}) async-start(s8[9437184]{0:T(1024)(128)(4,1)} %bitcast.367), calls=%async_computation.38 | async-start | bytes 8388608 | tf_op jit(solution)/shard_map/cond
  265.0 3.0 slice-start.35
  273.1 0.7 copy-start.6
  286.0 9.4 %collective-permute-start.6 = (bf16[64,3072]{1,0:T(8,128)(2,1)S(1)}, bf16[64,3072]{1,0:T(8,128)(2,1)}, u32[]{:S(2)}, u32[]{:S(2)}) collective-permute-start(bf16[64,3072]{1,0:T(8,128)(2,1)S(1)} %get-tuple-element.413), channel_id=1, source_target_pairs={{3,0},{0,1},{1,2},{2,3},{7,4},{4,5},{5,6},{6,7},{11,8},{8,9},{9,10... | collective-permute-start | bytes 1179656 | tf_op jit(solution)/shard_map/ppermute | solution.py:17
  287.3 12.3 %collective-permute-start.7 = (bf16[32,3072]{1,0:T(8,128)(2,1)S(1)}, bf16[32,3072]{1,0:T(8,128)(2,1)S(1)}, u32[]{:S(2)}, u32[]{:S(2)}) collective-permute-start(bf16[32,3072]{1,0:T(8,128)(2,1)S(1)} %fusion.172), channel_id=1, source_target_pairs={{3,0},{0,1},{1,2},{2,3},{7,4},{4,5},{5,6},{6,7},{11,8},{8,9},{9,10... | collective-permute-start | bytes 589832 | tf_op jit(solution)/shard_map/ppermute | solution.py:17
  301.0 6.4 %slice-start.12 = ((s8[9437184]{0:T(1024)(128)(4,1)}), s8[4194304]{0:T(1024)(128)(4,1)S(1)}, s32[]{:S(2)}) async-start(s8[9437184]{0:T(1024)(128)(4,1)} %bitcast.353), calls=%async_computation.16 | async-start | bytes 8388608 | tf_op jit(solution)/shard_map/cond
  301.2 6.2 %slice-start.13 = ((s8[9437184]{0:T(1024)(128)(4,1)}), s8[4194304]{0:T(1024)(128)(4,1)S(1)}, s32[]{:S(2)}) async-start(s8[9437184]{0:T(1024)(128)(4,1)} %bitcast.353), calls=%async_computation.17 | async-start | bytes 8388608 | tf_op jit(solution)/shard_map/cond
  301.2 6.2 %slice-start.14 = ((s8[9437184]{0:T(1024)(128)(4,1)}), s8[1048576]{0:T(1024)(128)(4,1)S(1)}, s32[]{:S(2)}) async-start(s8[9437184]{0:T(1024)(128)(4,1)} %bitcast.353), calls=%async_computation.18 | async-start | bytes 2097152 | tf_op jit(solution)/shard_map/cond
  301.2 8.6 %slice-start.36 = ((s8[9437184]{0:T(1024)(128)(4,1)}), s8[4194304]{0:T(1024)(128)(4,1)S(1)}, s32[]{:S(2)}) async-start(s8[9437184]{0:T(1024)(128)(4,1)} %bitcast.369), calls=%async_computation.40 | async-start | bytes 8388608 | tf_op jit(solution)/shard_map/cond
  301.2 8.8 %slice-start.37 = ((s8[9437184]{0:T(1024)(128)(4,1)}), s8[4194304]{0:T(1024)(128)(4,1)S(1)}, s32[]{:S(2)}) async-start(s8[9437184]{0:T(1024)(128)(4,1)} %bitcast.369), calls=%async_computation.41 | async-start | bytes 8388608 | tf_op jit(solution)/shard_map/cond
  307.4 3.0 slice-start.38
  315.5 0.7 copy-start.7
  328.4 7.8 %collective-permute-start.8 = (bf16[64,3072]{1,0:T(8,128)(2,1)S(1)}, bf16[64,3072]{1,0:T(8,128)(2,1)}, u32[]{:S(2)}, u32[]{:S(2)}) collective-permute-start(bf16[64,3072]{1,0:T(8,128)(2,1)S(1)} %get-tuple-element.415), channel_id=1, source_target_pairs={{3,0},{0,1},{1,2},{2,3},{7,4},{4,5},{5,6},{6,7},{11,8},{8,9},{9,10... | collective-permute-start | bytes 1179656 | tf_op jit(solution)/shard_map/ppermute | solution.py:17
  331.1 9.3 %collective-permute-start.9 = (bf16[32,3072]{1,0:T(8,128)(2,1)S(1)}, bf16[32,3072]{1,0:T(8,128)(2,1)S(1)}, u32[]{:S(2)}, u32[]{:S(2)}) collective-permute-start(bf16[32,3072]{1,0:T(8,128)(2,1)S(1)} %fusion.171), channel_id=1, source_target_pairs={{3,0},{0,1},{1,2},{2,3},{7,4},{4,5},{5,6},{6,7},{11,8},{8,9},{9,10... | collective-permute-start | bytes 589832 | tf_op jit(solution)/shard_map/ppermute | solution.py:17
  341.6 30.8 %collective-permute-start.10 = (bf16[64,3072]{1,0:T(8,128)(2,1)S(1)}, bf16[64,3072]{1,0:T(8,128)(2,1)}, u32[]{:S(2)}, u32[]{:S(2)}) collective-permute-start(bf16[64,3072]{1,0:T(8,128)(2,1)S(1)} %get-tuple-element.417), channel_id=1, source_target_pairs={{3,0},{0,1},{1,2},{2,3},{7,4},{4,5},{5,6},{6,7},{11,8},{8,9},{9,10... | collective-permute-start | bytes 1179656 | tf_op jit(solution)/shard_map/ppermute | solution.py:17
  346.4 28.7 %collective-permute-start.11 = (bf16[32,3072]{1,0:T(8,128)(2,1)S(1)}, bf16[32,3072]{1,0:T(8,128)(2,1)S(1)}, u32[]{:S(2)}, u32[]{:S(2)}) collective-permute-start(bf16[32,3072]{1,0:T(8,128)(2,1)S(1)} %fusion.170), channel_id=1, source_target_pairs={{3,0},{0,1},{1,2},{2,3},{7,4},{4,5},{5,6},{6,7},{11,8},{8,9},{9,10... | collective-permute-start | bytes 589832 | tf_op jit(solution)/shard_map/ppermute | solution.py:17
  376.3 44.4 %collective-permute-start.12 = (bf16[64,3072]{1,0:T(8,128)(2,1)S(1)}, bf16[64,3072]{1,0:T(8,128)(2,1)}, u32[]{:S(2)}, u32[]{:S(2)}) collective-permute-start(bf16[64,3072]{1,0:T(8,128)(2,1)S(1)} %get-tuple-element.420), channel_id=1, source_target_pairs={{3,0},{0,1},{1,2},{2,3},{7,4},{4,5},{5,6},{6,7},{11,8},{8,9},{9,10... | collective-permute-start | bytes 1179656 | tf_op jit(solution)/shard_map/ppermute | solution.py:17
  382.1 37.9 %collective-permute-start.13 = (bf16[32,3072]{1,0:T(8,128)(2,1)S(1)}, bf16[32,3072]{1,0:T(8,128)(2,1)S(1)}, u32[]{:S(2)}, u32[]{:S(2)}) collective-permute-start(bf16[32,3072]{1,0:T(8,128)(2,1)S(1)} %fusion.169), channel_id=1, source_target_pairs={{3,0},{0,1},{1,2},{2,3},{7,4},{4,5},{5,6},{6,7},{11,8},{8,9},{9,10... | collective-permute-start | bytes 589832 | tf_op jit(solution)/shard_map/ppermute | solution.py:17
  420.0 0.7 copy-start.10
  424.1 5.7 %slice-start.21 = ((s8[9437184]{0:T(1024)(128)(4,1)}), s8[4194304]{0:T(1024)(128)(4,1)S(1)}, s32[]{:S(2)}) async-start(s8[9437184]{0:T(1024)(128)(4,1)} %bitcast.359), calls=%async_computation.25 | async-start | bytes 8388608 | tf_op jit(solution)/shard_map/cond
  424.3 6.0 %slice-start.22 = ((s8[9437184]{0:T(1024)(128)(4,1)}), s8[4194304]{0:T(1024)(128)(4,1)S(1)}, s32[]{:S(2)}) async-start(s8[9437184]{0:T(1024)(128)(4,1)} %bitcast.359), calls=%async_computation.26 | async-start | bytes 8388608 | tf_op jit(solution)/shard_map/cond
  424.3 6.2 %slice-start.23 = ((s8[9437184]{0:T(1024)(128)(4,1)}), s8[1048576]{0:T(1024)(128)(4,1)S(1)}, s32[]{:S(2)}) async-start(s8[9437184]{0:T(1024)(128)(4,1)} %bitcast.359), calls=%async_computation.27 | async-start | bytes 2097152 | tf_op jit(solution)/shard_map/cond
  424.3 7.8 %slice-start.45 = ((s8[9437184]{0:T(1024)(128)(4,1)}), s8[4194304]{0:T(1024)(128)(4,1)S(1)}, s32[]{:S(2)}) async-start(s8[9437184]{0:T(1024)(128)(4,1)} %bitcast.375), calls=%async_computation.49 | async-start | bytes 8388608 | tf_op jit(solution)/shard_map/cond
  424.3 8.7 %slice-start.46 = ((s8[9437184]{0:T(1024)(128)(4,1)}), s8[4194304]{0:T(1024)(128)(4,1)S(1)}, s32[]{:S(2)}) async-start(s8[9437184]{0:T(1024)(128)(4,1)} %bitcast.375), calls=%async_computation.50 | async-start | bytes 8388608 | tf_op jit(solution)/shard_map/cond
  430.5 2.8 slice-start.47
Sparse Core Ops, SparseCore 0:
  10.0 60.2 all-gather.2
  72.1 58.8 all-gather.4
  458.9 80.0 reduce-scatter.3
where the time goes:
time: 560 us; the launch traced here: 552 us
  waiting for transfers between devices  281 us (50%)
  starting transfers between devices  129 us (23%)
  matrix products  58 us (10%)
  local copies, waits for them, and re-layouts  37.6 us (7%)
  between operations  23.3 us (4%)
  other arithmetic  19.7 us (4%)
    ppermute x14, starting transfers between devices, passed_along(): return lax.ppermute(block, axis, route)  129 us
    ppermute x14, waiting for transfers between devices, passed_along(): return lax.ppermute(block, axis, route)  81.6 us
    unnamed x4, waiting for transfers between devices  81 us
    all_gather x1, waiting for transfers between devices, local(): lax.all_gather(w_qk[0][:, heads_width:], 'dp', axis=0, tiled=True)  60.7 us
    all_gather x1, waiting for transfers between devices, local(): lax.all_gather(w_qk[0][:, :heads_width], 'dp', axis=0, tiled=True)  57.5 us
    dot_general x3, matrix products, attend(): jnp.dot(normed, weights_v, preferred_element_type=jnp.float32)  17.8 us
    unnamed x14, local copies, waits for them, and re-layouts  15.7 us
    dot_general x2, matrix products, attend(): lax.dot_general(mixed_heads, weights_out, (((1,), (1,)), ((), ())), prefe...  13.3 us
  transfers between devices with their start and end apart: 17, of which 15 were waited for; matrix products, arithmetic and copies ran while one was open for 1% of the time, Pallas kernels for 0%

commit v1 on v0

--- a/solution.py
+++ b/solution.py
@@ -1,7 +1,11 @@
+import functools
+
 import jax
 import jax.numpy as jnp
 import numpy as np
 from jax import lax
+from jax.experimental import pallas as pl
+from jax.experimental.pallas import tpu as pltpu
 from jax.sharding import PartitionSpec as P
 
 HEADS = 12
@@ -9,6 +13,8 @@
 TILE = 64
 MB = 3
 LAG = 2
+CHUNKS = 4
+MESH = pl.DeviceIdType.MESH
 
 
 def passed_along(block, axis, distance):
@@ -127,6 +133,457 @@
     return gradient[None]
 
 
+def chip_neighbours(dp):
+    core = dp % 2
+    x = (dp // 2) % 2
+    y = dp // 4
+    sibling = dp + 1 - 2 * core
+    along_x = y * 4 + (1 - x) * 2 + core
+    along_y = (1 - y) * 4 + x * 2 + core
+    across = (1 - y) * 4 + (1 - x) * 2 + core
+    return sibling, along_x, along_y, across
+
+
+def dot_nn(a, b):
+    return jnp.dot(a, b, preferred_element_type=jnp.float32)
+
+
+def dot_nt(a, b):
+    return lax.dot_general(a, b, (((1,), (1,)), ((), ())), preferred_element_type=jnp.float32)
+
+
+def dot_tn(a, b):
+    return lax.dot_general(a, b, (((0,), (0,)), ((), ())), preferred_element_type=jnp.float32)
+
+
+def row_scale(rows):
+    wide = rows.astype(jnp.float32)
+    return lax.rsqrt(jnp.mean(wide * wide, axis=-1, keepdims=True) + 1e-06)
+
+
+def fused(
+    n_dp, n_pipe, latents, cache, w_qk, w_v, w_out, bias, cot, out,
+    wq, wk, wv, wo, given, hid, outgo, ctx2, qacc, kacc, vacc, qb, kb, vb, o_all, ct_all,
+    ld_sem, w_send, w_recv, h_send, h_recv, c_send, c_recv, o_send, o_recv, t_send, t_recv,
+):
+    dp = lax.axis_index("dp")
+    stage = lax.axis_index("pipe")
+    sibling, along_x, along_y, across = chip_neighbours(dp)
+    tok = latents.shape[1]
+    ctx = cache.shape[1]
+    width = latents.shape[2]
+    heads_width = w_v.shape[1]
+    shard = w_qk.shape[0]
+    step = width // CHUNKS
+    last = n_pipe - 1
+    base = LAG * ctx
+
+    loads = [
+        pltpu.make_async_copy(cache.at[m], given.at[pl.ds(m * ctx, ctx)], ld_sem.at[m])
+        for m in range(LAG)
+    ]
+    loads += [
+        pltpu.make_async_copy(latents.at[m], given.at[pl.ds(base + m * tok, tok)], ld_sem.at[LAG + m])
+        for m in range(MB)
+    ]
+    load_v = pltpu.make_async_copy(w_v, wv, ld_sem.at[LAG + MB])
+    load_o = pltpu.make_async_copy(w_out, wo, ld_sem.at[LAG + MB + 1])
+    own_rows = pl.ds(pl.multiple_of(dp * shard, shard), shard)
+    own_q = pltpu.make_async_copy(
+        w_qk.at[:, pl.ds(0, heads_width)], wq.at[own_rows], ld_sem.at[LAG + MB + 2]
+    )
+    own_k = pltpu.make_async_copy(
+        w_qk.at[:, pl.ds(heads_width, heads_width)], wk.at[own_rows], ld_sem.at[LAG + MB + 3]
+    )
+    own_t = pltpu.make_async_copy(
+        cot.at[:, :, pl.ds(pl.multiple_of(dp * shard, shard), shard)],
+        ct_all.at[:, dp],
+        ld_sem.at[LAG + MB + 4],
+    )
+    for copy in loads:
+        copy.start()
+    load_v.start()
+
+    barrier = pltpu.get_barrier_semaphore()
+    for k in range(1, n_dp):
+        pl.semaphore_signal(barrier, 1, device_id=((dp + k) % n_dp, stage), device_id_type=MESH)
+    for k in range(1, n_pipe):
+        pl.semaphore_signal(barrier, 1, device_id=(dp, (stage + k) % n_pipe), device_id_type=MESH)
+    pl.semaphore_wait(barrier, n_dp - 1 + n_pipe - 1)
+
+    halves = (wq, wk)
+    sent = []
+
+    def rows_of(j):
+        return pl.ds(pl.multiple_of(j * shard, shard), shard)
+
+    def send_own(half, target):
+        copy = pltpu.make_async_remote_copy(
+            src_ref=w_qk.at[:, pl.ds(half * heads_width, heads_width)],
+            dst_ref=halves[half].at[own_rows],
+            send_sem=w_send.at[len(sent)],
+            recv_sem=w_recv.at[dp, half],
+            device_id=(target, stage),
+            device_id_type=MESH,
+        )
+        copy.start()
+        sent.append(copy)
+
+    def piece(j, half, target, slot):
+        ref = halves[half].at[rows_of(j)]
+        return pltpu.make_async_remote_copy(
+            src_ref=ref,
+            dst_ref=ref,
+            send_sem=w_send.at[slot],
+            recv_sem=w_recv.at[j, half],
+            device_id=(target, stage),
+            device_id_type=MESH,
+        )
+
+    def forward(j, half, target):
+        copy = piece(j, half, target, len(sent))
+        copy.start()
+        sent.append(copy)
+
+    def arrived(j, half):
+        piece(j, half, sibling, 0).wait_recv()
+
+    send_own(0, along_y)
+    send_own(1, along_x)
+    send_own(1, along_y)
+    send_own(0, along_x)
+    send_own(0, sibling)
+    send_own(1, sibling)
+    own_q.start()
+    own_k.start()
+    load_o.start()
+    own_t.start()
+
+    for copy in loads:
+        copy.wait()
+    load_v.wait()
+    tile = heads_width // 6
+
+    @pl.loop(0, 6)
+    def _(n):
+        cols = pl.ds(pl.multiple_of(n * tile, tile), tile)
+        vacc[:, cols] = dot_nn(given[...], wv[:, cols])
+
+    qacc[...] = jnp.zeros_like(qacc)
+    kacc[...] = jnp.zeros_like(kacc)
+
+    @pl.when(stage == 0)
+    def _():
+        for m in range(MB):
+            hid[m] = given[base + m * tok : base + (m + 1) * tok]
+
+    wide = heads_width // 3
+
+    def use(j, half):
+        acc = (qacc, kacc)[half]
+        weights = halves[half]
+        first = base if half == 0 else 0
+
+        @pl.loop(0, 3)
+        def _(n):
+            cols = pl.ds(pl.multiple_of(n * wide, wide), wide)
+            acc[first:, cols] += dot_nn(given[first:, rows_of(j)], weights[rows_of(j), cols])
+
+    own_q.wait()
+    use(dp, 0)
+    own_k.wait()
+    use(dp, 1)
+    arrived(sibling, 0)
+    use(sibling, 0)
+    arrived(sibling, 1)
+    use(sibling, 1)
+    arrived(along_y, 0)
+    forward(along_y, 0, along_x)
+    forward(along_y, 0, sibling)
+    arrived(along_x, 1)
+    forward(along_x, 1, along_y)
+    forward(along_x, 1, sibling)
+    use(along_y, 0)
+    use(along_x, 1)
+    arrived(along_y, 1)
+    forward(along_y, 1, sibling)
+    arrived(along_x, 0)
+    forward(along_x, 0, sibling)
+    use(along_y, 1)
+    use(along_x, 0)
+    sib_x, sib_y, sib_d = [
+        neighbour + 1 - 2 * (dp % 2) for neighbour in (along_x, along_y, across)
+    ]
+    for j in (sib_y, sib_x):
+        for half in range(2):
+            arrived(j, half)
+            use(j, half)
+    for half in range(2):
+        arrived(across, half)
+        forward(across, half, sibling)
+    for half in range(2):
+        use(across, half)
+    for half in range(2):
+        arrived(sib_d, half)
+        use(sib_d, half)
+
+    cot_sent = []
+    own_t.wait()
+    for k in range(1, n_dp):
+        target = (dp + k) % n_dp
+        copy = pltpu.make_async_remote_copy(
+            src_ref=cot.at[:, :, pl.ds(pl.multiple_of(target * shard, shard), shard)],
+            dst_ref=ct_all.at[:, dp],
+            send_sem=t_send.at[k],
+            recv_sem=t_recv.at[dp],
+            device_id=(target, stage),
+            device_id_type=MESH,
+        )
+        copy.start()
+        cot_sent.append(copy)
+
+    load_o.wait()
+    scale = row_scale(given[0:base])
+    for m in range(LAG):
+        rows = slice(m * ctx, (m + 1) * ctx)
+        kb[m, 0:ctx] = (kacc[rows] * scale[rows]).astype(jnp.bfloat16)
+        vb[m, 0:ctx] = (vacc[rows] * scale[rows]).astype(jnp.bfloat16)
+
+    def hop(m, c, target):
+        cols = pl.ds(c * step, step)
+        return pltpu.make_async_remote_copy(
+            src_ref=outgo.at[m, :, cols],
+            dst_ref=hid.at[m, :, cols],
+            send_sem=h_send.at[m, c],
+            recv_sem=h_recv.at[m, c],
+            device_id=(dp, target),
+            device_id_type=MESH,
+        )
+
+    def loop_back(c, target, slot):
+        ref = ctx2.at[:, pl.ds(c * step, step)]
+        return pltpu.make_async_remote_copy(
+            src_ref=ref,
+            dst_ref=ref,
+            send_sem=c_send.at[slot, c],
+            recv_sem=c_recv.at[c],
+            device_id=(dp, target),
+            device_id_type=MESH,
+        )
+
+    def spread(m, k):
+        target = (dp + k) % n_dp
+        ref = o_all.at[m, dp]
+        return pltpu.make_async_remote_copy(
+            src_ref=ref,
+            dst_ref=ref,
+            send_sem=o_send.at[m, k],
+            recv_sem=o_recv.at[m, dp],
+            device_id=(target, stage),
+            device_id_type=MESH,
+        )
+
+    def contract(rows, lhs, c, pairs):
+        for acc, weights in pairs:
+            @pl.loop(0, 3)
+            def _(n):
+                cols = pl.ds(pl.multiple_of(n * wide, wide), wide)
+                term = dot_nn(lhs, weights[c * step : (c + 1) * step, cols])
+                if c == 0:
+                    acc[rows, cols] = term
+                else:
+                    acc[rows, cols] += term
+
+    def process(m):
+        rows = slice(base + m * tok, base + (m + 1) * tok)
+        if m >= LAG:
+            for c in range(CHUNKS):
+                @pl.when(stage != last)
+                def _():
+                    loop_back(c, last, 0).wait_recv()
+
+                contract(
+                    slice(0, ctx), ctx2[:, c * step : (c + 1) * step], c, ((kacc, wk), (vacc, wv))
+                )
+            scale = row_scale(ctx2[...])
+            kb[m, 0:ctx] = (kacc[0:ctx] * scale).astype(jnp.bfloat16)
+            vb[m, 0:ctx] = (vacc[0:ctx] * scale).astype(jnp.bfloat16)
+
+        @pl.when(stage > 0)
+        def _():
+            for c in range(CHUNKS):
+                hop(m, c, (stage + 1) % n_pipe).wait_recv()
+                contract(
+                    rows,
+                    hid[m, :, c * step : (c + 1) * step],
+                    c,
+                    ((qacc, wq), (kacc, wk), (vacc, wv)),
+                )
+
+        scale = row_scale(hid[m])
+        qb[...] = (qacc[rows] * scale).astype(jnp.bfloat16)
+        kb[m, ctx:] = (kacc[rows] * scale).astype(jnp.bfloat16)
+        vb[m, ctx:] = (vacc[rows] * scale).astype(jnp.bfloat16)
+        heads = [slice(h * HDIM, (h + 1) * HDIM) for h in range(HEADS)]
+        scores = jnp.concatenate([dot_nt(qb[:, s], kb[m, :, s]) for s in heads], axis=0)
+        scores = scores * HDIM ** (-0.5) + bias[m : m + 1, :]
+        largest = jnp.max(scores, axis=-1, keepdims=True)
+        exponent = jnp.exp(scores - largest)
+        attention = (exponent / jnp.sum(exponent, axis=-1, keepdims=True)).astype(jnp.bfloat16)
+        for h, s in enumerate(heads):
+            o_all[m, dp, :, s] = dot_nn(
+                attention[h * tok : (h + 1) * tok], vb[m, :, s]
+            ).astype(jnp.bfloat16)
+        if m == MB - 1:
+            for k in range(1, n_dp):
+                spread(m, k).start()
+
+        @pl.when(stage != last)
+        def _():
+            for c in range(CHUNKS):
+                cols = slice(c * step, (c + 1) * step)
+                outgo[m, :, cols] = (
+                    hid[m, :, cols].astype(jnp.float32) + dot_nt(o_all[m, dp], wo[cols, :])
+                ).astype(jnp.bfloat16)
+                hop(m, c, (stage + 1) % n_pipe).start()
+
+        if m + LAG < MB:
+            @pl.when(stage == last)
+            def _():
+                for c in range(CHUNKS):
+                    cols = slice(c * step, (c + 1) * step)
+                    ctx2[:, cols] = (
+                        hid[m, tok - ctx :, cols].astype(jnp.float32)
+                        + dot_nt(o_all[m, dp, tok - ctx :, :], wo[cols, :])
+                    ).astype(jnp.bfloat16)
+                    loop_back(c, 0, 0).start()
+                for target in range(1, n_pipe - 1):
+                    for c in range(CHUNKS):
+                        loop_back(c, target, target).start()
+
+        if m < MB - 1:
+            for k in range(1, n_dp):
+                spread(m, k).start()
+
+    def gradient(m):
+        if m == 0:
+            for k in range(1, n_dp):
+                source = (dp + k) % n_dp
+                pltpu.make_async_remote_copy(
+                    src_ref=ct_all.at[:, source],
+                    dst_ref=ct_all.at[:, source],
+                    send_sem=t_send.at[k],
+                    recv_sem=t_recv.at[source],
+                    device_id=(source, stage),
+                    device_id_type=MESH,
+                ).wait_recv()
+        for k in range(1, n_dp):
+            source = (dp + k) % n_dp
+            pltpu.make_async_remote_copy(
+                src_ref=o_all.at[m, source],
+                dst_ref=o_all.at[m, source],
+                send_sem=o_send.at[m, k],
+                recv_sem=o_recv.at[m, source],
+                device_id=(source, stage),
+                device_id_type=MESH,
+            ).wait_recv()
+
+        left = ct_all[m].reshape(n_dp * tok, shard)
+
+        @pl.loop(0, 3)
+        def _(n):
+            cols = pl.ds(pl.multiple_of(n * wide, wide), wide)
+            term = dot_tn(left, o_all[m, :, :, cols].reshape(n_dp * tok, wide))
+            if m == 0:
+                out[:, cols] = term
+            else:
+                out[:, cols] += term
+
+    for m in range(MB - 1):
+        process(m)
+    for m in range(MB - 1):
+        gradient(m)
+    process(MB - 1)
+    gradient(MB - 1)
+
+    for copy in sent + cot_sent:
+        copy.wait_send()
+    for m in range(MB):
+        for k in range(1, n_dp):
+            spread(m, k).wait_send()
+
+    @pl.when(stage != last)
+    def _():
+        for m in range(MB):
+            for c in range(CHUNKS):
+                hop(m, c, (stage + 1) % n_pipe).wait_send()
+
+    @pl.when(stage == last)
+    def _():
+        for target in range(n_pipe - 1):
+            for c in range(CHUNKS):
+                loop_back(c, target, target).wait_send()
+
+
+def local_fused(latents_in, context_cache, w_qk, w_v, w_out, tile_mask, out_cotangent):
+    n_dp = lax.axis_size("dp")
+    n_pipe = lax.axis_size("pipe")
+    tok, width = latents_in.shape[1:]
+    ctx = context_cache.shape[1]
+    heads_width = w_v.shape[2]
+    shard = w_qk.shape[1]
+    allowed = jnp.concatenate(
+        [jnp.repeat(tile_mask[:, 0, :1], ctx, axis=1), jnp.repeat(tile_mask[:, 0, 1:], tok, axis=1)],
+        axis=1,
+    )
+    bias = jnp.where(allowed == 1, 0.0, -1e30).astype(jnp.float32)
+    rows = LAG * ctx + MB * tok
+    keys = ctx + tok
+    bf, f32 = jnp.bfloat16, jnp.float32
+    dma = pltpu.SemaphoreType.DMA
+    anywhere = pl.BlockSpec(memory_space=pl.ANY)
+    vmem = pl.BlockSpec(memory_space=pltpu.VMEM)
+    out = pl.pallas_call(
+        functools.partial(fused, n_dp, n_pipe),
+        out_shape=jax.ShapeDtypeStruct((shard, heads_width), f32),
+        in_specs=[anywhere] * 5 + [vmem, anywhere],
+        out_specs=vmem,
+        scratch_shapes=[
+            pltpu.VMEM((width, heads_width), bf),
+            pltpu.VMEM((width, heads_width), bf),
+            pltpu.VMEM((width, heads_width), bf),
+            pltpu.VMEM((width, heads_width), bf),
+            pltpu.VMEM((rows, width), bf),
+            pltpu.VMEM((MB, tok, width), bf),
+            pltpu.VMEM((MB, tok, width), bf),
+            pltpu.VMEM((ctx, width), bf),
+            pltpu.VMEM((rows, heads_width), f32),
+            pltpu.VMEM((rows, heads_width), f32),
+            pltpu.VMEM((rows, heads_width), f32),
+            pltpu.VMEM((tok, heads_width), bf),
+            pltpu.VMEM((MB, keys, heads_width), bf),
+            pltpu.VMEM((MB, keys, heads_width), bf),
+            pltpu.VMEM((MB, n_dp, tok, heads_width), bf),
+            pltpu.VMEM((MB, n_dp, tok, shard), bf),
+            dma((LAG + MB + 5,)),
+            dma((14,)),
+            dma((n_dp, 2)),
+            dma((MB, CHUNKS)),
+            dma((MB, CHUNKS)),
+            dma((n_pipe - 1, CHUNKS)),
+            dma((CHUNKS,)),
+            dma((MB, n_dp)),
+            dma((MB, n_dp)),
+            dma((n_dp,)),
+            dma((n_dp,)),
+        ],
+        compiler_params=pltpu.CompilerParams(
+            collective_id=0, has_side_effects=True, vmem_limit_bytes=62 * 2**20
+        ),
+    )(latents_in, context_cache, w_qk[0], w_v[0], w_out[0], bias, out_cotangent[0])
+    return out[None]
+
+
 def solution(mesh):
     in_specs = (
         P(None, "dp", None),
@@ -138,4 +595,6 @@
         P("pipe", None, "dp", None),
     )
     out_specs = P("pipe", "dp", None)
-    return jax.shard_map(local, mesh=mesh, in_specs=in_specs, out_specs=out_specs, check_vma=False)
+    fits = mesh.shape["dp"] == 8 and mesh.shape["pipe"] > 1
+    body = local_fused if fits else local
+    return jax.shard_map(body, mesh=mesh, in_specs=in_specs, out_specs=out_specs, check_vma=False)

time: 560 us -> 216 us (0.39); the launches traced: 552 us -> 216 us
  waiting for transfers between devices: 281 us -> 0 us
  Pallas kernels: 0 us -> 211 us
  starting transfers between devices: 129 us -> 0 us
  matrix products: 58 us -> 0 us
  local copies, waits for them, and re-layouts: 37.6 us -> 4.12 us
  between operations: 23.3 us -> 0.01 us
  other arithmetic: 19.7 us -> 0.65 us
    pallas_call x0 -> x1, Pallas kernels: none -> 211 us  [local_fused(): pl.pallas_call(functools.partial(fused, n_dp, n_pipe), out_shape=jax.Shap...]
    ppermute x14 -> x0, starting transfers between devices: 129 us -> none  [passed_along(): return lax.ppermute(block, axis, route)]
    all_gather x2 -> x0, waiting for transfers between devices: 118 us -> none  [the longest x1 60.7 us: local(): lax.all_gather(w_qk[0][:, heads_width:], 'dp', axis=0, tiled=True)]
    ppermute x14 -> x0, waiting for transfers between devices: 81.6 us -> none  [passed_along(): return lax.ppermute(block, axis, route)]
    unnamed x4 -> x0, waiting for transfers between devices: 81 us -> none
    dot_general x18 -> x0, matrix products: 58 us -> none  [the longest x3 17.8 us: attend(): jnp.dot(normed, weights_v, preferred_element_type=jnp.float32)]
    select_n x16 -> x1, other arithmetic: 14.2 us -> 0.65 us  [local_fused(): bias = jnp.where(allowed == 1, 0.0, -1e+30).astype(jnp.float32)]
    unnamed x14 -> x1, local copies, waits for them, and re-layouts: 15.7 us -> 3.22 us
  transfers between devices with their start and end apart: 17 -> 0, of which waited for: 15 -> 0; matrix products, arithmetic and copies ran while one was open for 1% -> 0% of each run, Pallas kernels for 0% -> 0%
where the time goes in v1:
time: 216 us
  Pallas kernels  211 us (98%)
  local copies, waits for them, and re-layouts  4.12 us (2%)
    pallas_call x1, Pallas kernels, local_fused(): pl.pallas_call(functools.partial(fused, n_dp, n_pipe), out_shape=jax.Shap...  211 us

profile of v1, /device:TPU:25, one launch (start us, length us, event | category | flops | bytes accessed | tf_op | source)
XLA Modules:
  0.0 216.0 jit_solution(8408242377545746785)
XLA Ops:
  0.0 0.8 slice_bitcast_fusion.1
  0.8 0.1 reshape.10
  0.8 0.1 reshape.11
  0.9 0.7 fusion.bias
  1.6 211.2 %shard_map.73 = f32[384,1536]{1,0:T(8,128)} custom-call(bf16[3,64,3072]{2,1,0:T(8,128)(2,1)} %latents.1, bf16[2,32,3072]{2,1,0:T(8,128)(2,1)} %cache.1, bf16[384,3072]{1,0:T(8,128)(2,1)} %bitcast.12, bf16[3072,1536]{1,0:T(8,128)(2,1)} %bitcast.9, bf16[3072,1536]{1,0:T(8,128)(2,1)} %bitcast.10, f32[3,96]{1,0:T(4,128)} %fusion.bias, bf16[3,64,3072]{2,1,0:T(8,128)(2,1)} %bitcast.13), custom_call_target="tpu_custom_call" | custom-call | tf_op jit(solution)/shard_map/pallas_call | solution.py:546
  212.7 3.2 %copy.9 = f32[1,384,1536]{2,1,0:T(8,128)} copy(f32[1,384,1536]{2,1,0:T(8,128)} %bitcast.11) | data formatting | bytes 4718592

commit v2 on v1

--- a/solution.py
+++ b/solution.py
@@ -13,7 +13,8 @@
 TILE = 64
 MB = 3
 LAG = 2
-CHUNKS = 4
+PARTS = (1, 2, 3, 3, 2, 1)
+CHUNKS = len(PARTS)
 MESH = pl.DeviceIdType.MESH
 
 
@@ -164,7 +165,7 @@
 def fused(
     n_dp, n_pipe, latents, cache, w_qk, w_v, w_out, bias, cot, out,
     wq, wk, wv, wo, given, hid, outgo, ctx2, qacc, kacc, vacc, qb, kb, vb, o_all, ct_all,
-    ld_sem, w_send, w_recv, h_send, h_recv, c_send, c_recv, o_send, o_recv, t_send, t_recv,
+    ld_sem, w_send, w_recv, h_send, h_recv, c_send, c_recv, o_send, o_recv, t_send, t_recv, e_send, e_recv,
 ):
     dp = lax.axis_index("dp")
     stage = lax.axis_index("pipe")
@@ -174,7 +175,8 @@
     width = latents.shape[2]
     heads_width = w_v.shape[1]
     shard = w_qk.shape[0]
-    step = width // CHUNKS
+    unit = width // sum(PARTS)
+    edges = [unit * sum(PARTS[:c]) for c in range(CHUNKS + 1)]
     last = n_pipe - 1
     base = LAG * ctx
 
@@ -327,21 +329,6 @@
         arrived(sib_d, half)
         use(sib_d, half)
 
-    cot_sent = []
-    own_t.wait()
-    for k in range(1, n_dp):
-        target = (dp + k) % n_dp
-        copy = pltpu.make_async_remote_copy(
-            src_ref=cot.at[:, :, pl.ds(pl.multiple_of(target * shard, shard), shard)],
-            dst_ref=ct_all.at[:, dp],
-            send_sem=t_send.at[k],
-            recv_sem=t_recv.at[dp],
-            device_id=(target, stage),
-            device_id_type=MESH,
-        )
-        copy.start()
-        cot_sent.append(copy)
-
     load_o.wait()
     scale = row_scale(given[0:base])
     for m in range(LAG):
@@ -350,7 +337,7 @@
         vb[m, 0:ctx] = (vacc[rows] * scale[rows]).astype(jnp.bfloat16)
 
     def hop(m, c, target):
-        cols = pl.ds(c * step, step)
+        cols = pl.ds(edges[c], edges[c + 1] - edges[c])
         return pltpu.make_async_remote_copy(
             src_ref=outgo.at[m, :, cols],
             dst_ref=hid.at[m, :, cols],
@@ -361,7 +348,7 @@
         )
 
     def loop_back(c, target, slot):
-        ref = ctx2.at[:, pl.ds(c * step, step)]
+        ref = ctx2.at[:, pl.ds(edges[c], edges[c + 1] - edges[c])]
         return pltpu.make_async_remote_copy(
             src_ref=ref,
             dst_ref=ref,
@@ -383,16 +370,52 @@
             device_id_type=MESH,
         )
 
+    tail_sent = []
+
+    def tail_piece(j, half, target, slot):
+        ref = o_all.at[MB - 1, j, :, pl.ds(half * (heads_width // 2), heads_width // 2)]
+        return pltpu.make_async_remote_copy(
+            src_ref=ref,
+            dst_ref=ref,
+            send_sem=e_send.at[slot],
+            recv_sem=e_recv.at[j, half],
+            device_id=(target, stage),
+            device_id_type=MESH,
+        )
+
+    def tail_send(j, half, target):
+        copy = tail_piece(j, half, target, len(tail_sent))
+        copy.start()
+        tail_sent.append(copy)
+
+    def tail_arrived(j, half):
+        tail_piece(j, half, sibling, 0).wait_recv()
+
+    def finish_exchange():
+        tail_arrived(along_y, 0)
+        tail_send(along_y, 0, along_x)
+        tail_arrived(along_x, 1)
+        tail_send(along_x, 1, along_y)
+        tail_send(along_y, 0, sibling)
+        tail_send(along_x, 1, sibling)
+        tail_arrived(along_y, 1)
+        tail_send(along_y, 1, sibling)
+        tail_arrived(along_x, 0)
+        tail_send(along_x, 0, sibling)
+        for half in range(2):
+            tail_arrived(across, half)
+            tail_send(across, half, sibling)
+        for j in (sibling, sib_y, sib_x, sib_d):
+            for half in range(2):
+                tail_arrived(j, half)
+
     def contract(rows, lhs, c, pairs):
         for acc, weights in pairs:
-            @pl.loop(0, 3)
-            def _(n):
-                cols = pl.ds(pl.multiple_of(n * wide, wide), wide)
-                term = dot_nn(lhs, weights[c * step : (c + 1) * step, cols])
-                if c == 0:
-                    acc[rows, cols] = term
-                else:
-                    acc[rows, cols] += term
+            term = dot_nn(lhs, weights[edges[c] : edges[c + 1], :])
+            if c == 0:
+                acc[rows] = term
+            else:
+                acc[rows] += term
 
     def process(m):
         rows = slice(base + m * tok, base + (m + 1) * tok)
@@ -403,7 +426,7 @@
                     loop_back(c, last, 0).wait_recv()
 
                 contract(
-                    slice(0, ctx), ctx2[:, c * step : (c + 1) * step], c, ((kacc, wk), (vacc, wv))
+                    slice(0, ctx), ctx2[:, edges[c] : edges[c + 1]], c, ((kacc, wk), (vacc, wv))
                 )
             scale = row_scale(ctx2[...])
             kb[m, 0:ctx] = (kacc[0:ctx] * scale).astype(jnp.bfloat16)
@@ -415,7 +438,7 @@
                 hop(m, c, (stage + 1) % n_pipe).wait_recv()
                 contract(
                     rows,
-                    hid[m, :, c * step : (c + 1) * step],
+                    hid[m, :, edges[c] : edges[c + 1]],
                     c,
                     ((qacc, wq), (kacc, wk), (vacc, wv)),
                 )
@@ -435,13 +458,15 @@
                 attention[h * tok : (h + 1) * tok], vb[m, :, s]
             ).astype(jnp.bfloat16)
         if m == MB - 1:
-            for k in range(1, n_dp):
-                spread(m, k).start()
+            for half, target in ((0, along_y), (1, along_x), (1, along_y), (0, along_x)):
+                tail_send(dp, half, target)
+            for half in range(2):
+                tail_send(dp, half, sibling)
 
         @pl.when(stage != last)
         def _():
             for c in range(CHUNKS):
-                cols = slice(c * step, (c + 1) * step)
+                cols = slice(edges[c], edges[c + 1])
                 outgo[m, :, cols] = (
                     hid[m, :, cols].astype(jnp.float32) + dot_nt(o_all[m, dp], wo[cols, :])
                 ).astype(jnp.bfloat16)
@@ -451,12 +476,14 @@
             @pl.when(stage == last)
             def _():
                 for c in range(CHUNKS):
-                    cols = slice(c * step, (c + 1) * step)
+                    cols = slice(edges[c], edges[c + 1])
                     ctx2[:, cols] = (
                         hid[m, tok - ctx :, cols].astype(jnp.float32)
                         + dot_nt(o_all[m, dp, tok - ctx :, :], wo[cols, :])
                     ).astype(jnp.bfloat16)
                     loop_back(c, 0, 0).start()
+                for c in range(CHUNKS):
+                    loop_back(c, 0, 0).wait_send()
                 for target in range(1, n_pipe - 1):
                     for c in range(CHUNKS):
                         loop_back(c, target, target).start()
@@ -477,16 +504,19 @@
                     device_id=(source, stage),
                     device_id_type=MESH,
                 ).wait_recv()
-        for k in range(1, n_dp):
-            source = (dp + k) % n_dp
-            pltpu.make_async_remote_copy(
-                src_ref=o_all.at[m, source],
-                dst_ref=o_all.at[m, source],
-                send_sem=o_send.at[m, k],
-                recv_sem=o_recv.at[m, source],
-                device_id=(source, stage),
-                device_id_type=MESH,
-            ).wait_recv()
+        if m == MB - 1:
+            finish_exchange()
+        else:
+            for k in range(1, n_dp):
+                source = (dp + k) % n_dp
+                pltpu.make_async_remote_copy(
+                    src_ref=o_all.at[m, source],
+                    dst_ref=o_all.at[m, source],
+                    send_sem=o_send.at[m, k],
+                    recv_sem=o_recv.at[m, source],
+                    device_id=(source, stage),
+                    device_id_type=MESH,
+                ).wait_recv()
 
         left = ct_all[m].reshape(n_dp * tok, shard)
 
@@ -499,16 +529,31 @@
             else:
                 out[:, cols] += term
 
-    for m in range(MB - 1):
+    process(0)
+    cot_sent = []
+    own_t.wait()
+    for k in range(1, n_dp):
+        target = (dp + k) % n_dp
+        copy = pltpu.make_async_remote_copy(
+            src_ref=cot.at[:, :, pl.ds(pl.multiple_of(target * shard, shard), shard)],
+            dst_ref=ct_all.at[:, dp],
+            send_sem=t_send.at[k],
+            recv_sem=t_recv.at[dp],
+            device_id=(target, stage),
+            device_id_type=MESH,
+        )
+        copy.start()
+        cot_sent.append(copy)
+    for m in range(1, MB - 1):
         process(m)
     for m in range(MB - 1):
         gradient(m)
     process(MB - 1)
     gradient(MB - 1)
 
-    for copy in sent + cot_sent:
+    for copy in sent + cot_sent + tail_sent:
         copy.wait_send()
-    for m in range(MB):
+    for m in range(MB - 1):
         for k in range(1, n_dp):
             spread(m, k).wait_send()
 
@@ -520,7 +565,7 @@
 
     @pl.when(stage == last)
     def _():
-        for target in range(n_pipe - 1):
+        for target in range(1, n_pipe - 1):
             for c in range(CHUNKS):
                 loop_back(c, target, target).wait_send()
 
@@ -572,10 +617,12 @@
             dma((MB, CHUNKS)),
             dma((n_pipe - 1, CHUNKS)),
             dma((CHUNKS,)),
-            dma((MB, n_dp)),
-            dma((MB, n_dp)),
+            dma((MB - 1, n_dp)),
+            dma((MB - 1, n_dp)),
             dma((n_dp,)),
             dma((n_dp,)),
+            dma((14,)),
+            dma((n_dp, 2)),
         ],
         compiler_params=pltpu.CompilerParams(
             collective_id=0, has_side_effects=True, vmem_limit_bytes=62 * 2**20

time: 216 us -> 205 us (0.949)
  Pallas kernels: 211 us -> 199 us
    pallas_call x1, Pallas kernels: 211 us -> 199 us  [local_fused(): pl.pallas_call(functools.partial(fused, n_dp, n_pipe), out_shape=jax.Shap...]
where the time goes in v2:
time: 205 us; the launch traced here: 204 us
  Pallas kernels  199 us (97%)
  local copies, waits for them, and re-layouts  4.12 us (2%)
    pallas_call x1, Pallas kernels, local_fused(): pl.pallas_call(functools.partial(fused, n_dp, n_pipe), out_shape=jax.Shap...  199 us

profile of v2, /device:TPU:25, one launch (start us, length us, event | category | flops | bytes accessed | tf_op | source)
XLA Modules:
  0.0 204.3 jit_solution(16240863407902338500)
XLA Ops:
  0.0 0.8 slice_bitcast_fusion.1
  0.8 0.1 reshape.10
  0.8 0.1 reshape.11
  0.9 0.7 fusion.bias
  1.6 199.5 %shard_map.73 = f32[384,1536]{1,0:T(8,128)} custom-call(bf16[3,64,3072]{2,1,0:T(8,128)(2,1)} %latents.1, bf16[2,32,3072]{2,1,0:T(8,128)(2,1)} %cache.1, bf16[384,3072]{1,0:T(8,128)(2,1)} %bitcast.12, bf16[3072,1536]{1,0:T(8,128)(2,1)} %bitcast.9, bf16[3072,1536]{1,0:T(8,128)(2,1)} %bitcast.10, f32[3,96]{1,0:T(4,128)} %fusion.bias, bf16[3,64,3072]{2,1,0:T(8,128)(2,1)} %bitcast.13), custom_call_target="tpu_custom_call" | custom-call | tf_op jit(solution)/shard_map/pallas_call | solution.py:591
  201.0 3.2 %copy.9 = f32[1,384,1536]{2,1,0:T(8,128)} copy(f32[1,384,1536]{2,1,0:T(8,128)} %bitcast.11) | data formatting | bytes 4718592

commit v3 on v2

--- a/solution.py
+++ b/solution.py
@@ -163,8 +163,9 @@
 
 
 def fused(
-    n_dp, n_pipe, latents, cache, w_qk, w_v, w_out, bias, cot, out,
+    n_dp, n_pipe, latents, cache, w_qk, w_v, w_out, mask, cot, part, o_last, ct_last,
     wq, wk, wv, wo, given, hid, outgo, ctx2, qacc, kacc, vacc, qb, kb, vb, o_all, ct_all,
+    gsum,
     ld_sem, w_send, w_recv, h_send, h_recv, c_send, c_recv, o_send, o_recv, t_send, t_recv, e_send, e_recv,
 ):
     dp = lax.axis_index("dp")
@@ -372,10 +373,15 @@
 
     tail_sent = []
 
-    def tail_piece(j, half, target, slot):
-        ref = o_all.at[MB - 1, j, :, pl.ds(half * (heads_width // 2), heads_width // 2)]
+    own_o = pltpu.make_async_copy(o_all.at[MB - 1, dp], o_last.at[dp], ld_sem.at[LAG + MB + 5])
+    part_out = pltpu.make_async_copy(gsum, part, ld_sem.at[LAG + MB + 6])
+    ct_out = pltpu.make_async_copy(ct_all.at[MB - 1], ct_last, ld_sem.at[LAG + MB + 7])
+
+    def tail_piece(j, half, target, slot, own=False):
+        cols = pl.ds(half * (heads_width // 2), heads_width // 2)
+        ref = o_last.at[j, :, cols]
         return pltpu.make_async_remote_copy(
-            src_ref=ref,
+            src_ref=o_all.at[MB - 1, dp, :, cols] if own else ref,
             dst_ref=ref,
             send_sem=e_send.at[slot],
             recv_sem=e_recv.at[j, half],
@@ -383,8 +389,8 @@
             device_id_type=MESH,
         )
 
-    def tail_send(j, half, target):
-        copy = tail_piece(j, half, target, len(tail_sent))
+    def tail_send(j, half, target, own=False):
+        copy = tail_piece(j, half, target, len(tail_sent), own)
         copy.start()
         tail_sent.append(copy)
 
@@ -449,7 +455,9 @@
         vb[m, ctx:] = (vacc[rows] * scale).astype(jnp.bfloat16)
         heads = [slice(h * HDIM, (h + 1) * HDIM) for h in range(HEADS)]
         scores = jnp.concatenate([dot_nt(qb[:, s], kb[m, :, s]) for s in heads], axis=0)
-        scores = scores * HDIM ** (-0.5) + bias[m : m + 1, :]
+        in_context = lax.broadcasted_iota(jnp.int32, (1, ctx + tok), 1) < ctx
+        seen = jnp.where(in_context, mask[m, 0, 0], mask[m, 0, 1]).astype(jnp.float32)
+        scores = scores * HDIM ** (-0.5) + (seen - 1.0) * 1e30
         largest = jnp.max(scores, axis=-1, keepdims=True)
         exponent = jnp.exp(scores - largest)
         attention = (exponent / jnp.sum(exponent, axis=-1, keepdims=True)).astype(jnp.bfloat16)
@@ -459,9 +467,10 @@
             ).astype(jnp.bfloat16)
         if m == MB - 1:
             for half, target in ((0, along_y), (1, along_x), (1, along_y), (0, along_x)):
-                tail_send(dp, half, target)
+                tail_send(dp, half, target, True)
             for half in range(2):
-                tail_send(dp, half, sibling)
+                tail_send(dp, half, sibling, True)
+            own_o.start()
 
         @pl.when(stage != last)
         def _():
@@ -504,19 +513,16 @@
                     device_id=(source, stage),
                     device_id_type=MESH,
                 ).wait_recv()
-        if m == MB - 1:
-            finish_exchange()
-        else:
-            for k in range(1, n_dp):
-                source = (dp + k) % n_dp
-                pltpu.make_async_remote_copy(
-                    src_ref=o_all.at[m, source],
-                    dst_ref=o_all.at[m, source],
-                    send_sem=o_send.at[m, k],
-                    recv_sem=o_recv.at[m, source],
-                    device_id=(source, stage),
-                    device_id_type=MESH,
-                ).wait_recv()
+        for k in range(1, n_dp):
+            source = (dp + k) % n_dp
+            pltpu.make_async_remote_copy(
+                src_ref=o_all.at[m, source],
+                dst_ref=o_all.at[m, source],
+                send_sem=o_send.at[m, k],
+                recv_sem=o_recv.at[m, source],
+                device_id=(source, stage),
+                device_id_type=MESH,
+            ).wait_recv()
 
         left = ct_all[m].reshape(n_dp * tok, shard)
 
@@ -525,9 +531,9 @@
             cols = pl.ds(pl.multiple_of(n * wide, wide), wide)
             term = dot_tn(left, o_all[m, :, :, cols].reshape(n_dp * tok, wide))
             if m == 0:
-                out[:, cols] = term
+                gsum[:, cols] = term
             else:
-                out[:, cols] += term
+                gsum[:, cols] += term
 
     process(0)
     cot_sent = []
@@ -548,8 +554,12 @@
         process(m)
     for m in range(MB - 1):
         gradient(m)
+    part_out.start()
+    ct_out.start()
     process(MB - 1)
-    gradient(MB - 1)
+    finish_exchange()
+    for copy in (part_out, ct_out, own_o):
+        copy.wait()
 
     for copy in sent + cot_sent + tail_sent:
         copy.wait_send()
@@ -577,22 +587,20 @@
     ctx = context_cache.shape[1]
     heads_width = w_v.shape[2]
     shard = w_qk.shape[1]
-    allowed = jnp.concatenate(
-        [jnp.repeat(tile_mask[:, 0, :1], ctx, axis=1), jnp.repeat(tile_mask[:, 0, 1:], tok, axis=1)],
-        axis=1,
-    )
-    bias = jnp.where(allowed == 1, 0.0, -1e30).astype(jnp.float32)
     rows = LAG * ctx + MB * tok
     keys = ctx + tok
     bf, f32 = jnp.bfloat16, jnp.float32
     dma = pltpu.SemaphoreType.DMA
     anywhere = pl.BlockSpec(memory_space=pl.ANY)
-    vmem = pl.BlockSpec(memory_space=pltpu.VMEM)
-    out = pl.pallas_call(
+    part, o_last, ct_last = pl.pallas_call(
         functools.partial(fused, n_dp, n_pipe),
-        out_shape=jax.ShapeDtypeStruct((shard, heads_width), f32),
-        in_specs=[anywhere] * 5 + [vmem, anywhere],
-        out_specs=vmem,
+        out_shape=(
+            jax.ShapeDtypeStruct((shard, heads_width), f32),
+            jax.ShapeDtypeStruct((n_dp, tok, heads_width), bf),
+            jax.ShapeDtypeStruct((n_dp, tok, shard), bf),
+        ),
+        in_specs=[anywhere] * 5 + [pl.BlockSpec(memory_space=pltpu.SMEM), anywhere],
+        out_specs=(anywhere,) * 3,
         scratch_shapes=[
             pltpu.VMEM((width, heads_width), bf),
             pltpu.VMEM((width, heads_width), bf),
@@ -610,7 +618,8 @@
             pltpu.VMEM((MB, keys, heads_width), bf),
             pltpu.VMEM((MB, n_dp, tok, heads_width), bf),
             pltpu.VMEM((MB, n_dp, tok, shard), bf),
-            dma((LAG + MB + 5,)),
+            pltpu.VMEM((shard, heads_width), f32),
+            dma((LAG + MB + 8,)),
             dma((14,)),
             dma((n_dp, 2)),
             dma((MB, CHUNKS)),
@@ -627,8 +636,11 @@
         compiler_params=pltpu.CompilerParams(
             collective_id=0, has_side_effects=True, vmem_limit_bytes=62 * 2**20
         ),
-    )(latents_in, context_cache, w_qk[0], w_v[0], w_out[0], bias, out_cotangent[0])
-    return out[None]
+    )(latents_in, context_cache, w_qk[0], w_v[0], w_out[0], tile_mask, out_cotangent[0])
+    last_term = dot_tn(
+        ct_last.reshape(n_dp * tok, shard), o_last.reshape(n_dp * tok, heads_width)
+    )
+    return (part + last_term)[None]
 
 
 def solution(mesh):

time: 205 us -> 204 us (level)
  matrix products: 0 us -> 4.47 us
  local copies, waits for them, and re-layouts: 4.12 us -> 1.32 us
    dot_general x0 -> x1, matrix products: none -> 4.47 us  [dot_tn(): lax.dot_general(a, b, (((0,), (0,)), ((), ())), preferred_element_type=jn...]
where the time goes in v3:
time: 204 us
  Pallas kernels  198 us (97%)
  matrix products  4.47 us (2%)
    pallas_call x1, Pallas kernels, local_fused(): pl.pallas_call(functools.partial(fused, n_dp, n_pipe), out_shape=(jax.Sha...  198 us
    dot_general x1, matrix products, dot_tn(): lax.dot_general(a, b, (((0,), (0,)), ((), ())), preferred_element_type=jn...  4.47 us

profile of v3, /device:TPU:25, one launch (start us, length us, event | category | flops | bytes accessed | tf_op | source)
XLA Modules:
  0.0 204.2 jit_solution(13648232044126779711)
XLA Ops:
  0.0 1.3 copy.8.mask
  1.3 198.4 %shard_map.73 = (f32[384,1536]{1,0:T(8,128)}, bf16[8,64,1536]{2,1,0:T(8,128)(2,1)}, bf16[8,64,384]{2,1,0:T(8,128)(2,1)}) custom-call(bf16[3,64,3072]{2,1,0:T(8,128)(2,1)} %latents.1, bf16[2,32,3072]{2,1,0:T(8,128)(2,1)} %cache.1, bf16[384,3072]{1,0:T(8,128)(2,1)} %bitcast.16, bf16[3072,1536]{1,0:T(8,128)(2,1)} %bitcast.14, bf16[3072,1536]{1,0:T(8,128)(2,1)} %bitcast.15, ...), custom_call_target="tpu_custom_call" | custom-call | tf_op jit(solution)/shard_map/pallas_call | solution.py:595
  199.7 4.5 %fusion.1 = f32[1,384,1536]{2,1,0:T(8,128)} fusion(f32[384,1536]{1,0:T(8,128)} %get-tuple-element.8, bf16[8,64,384]{2,1,0:T(8,128)(2,1)} %get-tuple-element.9, bf16[8,64,1536]{2,1,0:T(8,128)(2,1)} %get-tuple-element.10), kind=kOutput, calls=%fused_computation.2 | convolution fusion | flops 604569600 | bytes 6684672 | tf_op jit(solution)/shard_map/dot_general | solution.py:157

commit v4 on v3

--- a/solution.py
+++ b/solution.py
@@ -465,13 +465,6 @@
             o_all[m, dp, :, s] = dot_nn(
                 attention[h * tok : (h + 1) * tok], vb[m, :, s]
             ).astype(jnp.bfloat16)
-        if m == MB - 1:
-            for half, target in ((0, along_y), (1, along_x), (1, along_y), (0, along_x)):
-                tail_send(dp, half, target, True)
-            for half in range(2):
-                tail_send(dp, half, sibling, True)
-            own_o.start()
-
         @pl.when(stage != last)
         def _():
             for c in range(CHUNKS):
@@ -500,6 +493,13 @@
         if m < MB - 1:
             for k in range(1, n_dp):
                 spread(m, k).start()
+
+        if m == MB - 1:
+            for half, target in ((0, along_y), (1, along_x), (1, along_y), (0, along_x)):
+                tail_send(dp, half, target, True)
+            for half in range(2):
+                tail_send(dp, half, sibling, True)
+            own_o.start()
 
     def gradient(m):
         if m == 0:

time: 204 us -> 204 us (level)
  no operation moved by 1% of the time
where the time goes in v4:
time: 204 us
  Pallas kernels  198 us (97%)
  matrix products  4.47 us (2%)
    pallas_call x1, Pallas kernels, local_fused(): pl.pallas_call(functools.partial(fused, n_dp, n_pipe), out_shape=(jax.Sha...  198 us
    dot_general x1, matrix products, dot_tn(): lax.dot_general(a, b, (((0,), (0,)), ((), ())), preferred_element_type=jn...  4.47 us

profile of v4, /device:TPU:25, one launch (start us, length us, event | category | flops | bytes accessed | tf_op | source)
XLA Modules:
  0.0 204.2 jit_solution(3124137324371037688)
XLA Ops:
  0.0 1.3 copy.8.mask
  1.3 198.4 %shard_map.73 = (f32[384,1536]{1,0:T(8,128)}, bf16[8,64,1536]{2,1,0:T(8,128)(2,1)}, bf16[8,64,384]{2,1,0:T(8,128)(2,1)}) custom-call(bf16[3,64,3072]{2,1,0:T(8,128)(2,1)} %latents.1, bf16[2,32,3072]{2,1,0:T(8,128)(2,1)} %cache.1, bf16[384,3072]{1,0:T(8,128)(2,1)} %bitcast.16, bf16[3072,1536]{1,0:T(8,128)(2,1)} %bitcast.14, bf16[3072,1536]{1,0:T(8,128)(2,1)} %bitcast.15, ...), custom_call_target="tpu_custom_call" | custom-call | tf_op jit(solution)/shard_map/pallas_call | solution.py:595
  199.8 4.5 %fusion.1 = f32[1,384,1536]{2,1,0:T(8,128)} fusion(f32[384,1536]{1,0:T(8,128)} %get-tuple-element.8, bf16[8,64,384]{2,1,0:T(8,128)(2,1)} %get-tuple-element.9, bf16[8,64,1536]{2,1,0:T(8,128)(2,1)} %get-tuple-element.10), kind=kOutput, calls=%fused_computation.2 | convolution fusion | flops 604569600 | bytes 6684672 | tf_op jit(solution)/shard_map/dot_general | solution.py:157
